TPU v7x, 32 devices: a whole 2x2x4 slice. The times are simulated.
32 devices in a mesh: groups: 2 (over y), gx: 4 (over z), gy: 4 (over x, core).
Axes of the slice: x: 2, y: 2, z: 4, core: 2. Of those that a mesh axis runs over, the one named last changes fastest.
Arguments:
- tokens: bfloat16 [2048, 8192], P(('groups', 'gy'), 'gx'), parts along dimension 0, may hold values from -70 to 70, as said below
- norm_gain: bfloat16 [8192], P('gx'), may hold values from 0.099609375 to 1.8984375
- w_query: bfloat16 [8192, 4096], P('gx', 'gy'), may hold values from -0.0625 to 0.0625
- w_key: bfloat16 [8192, 1024], P('gx', 'gy'), may hold values from -0.0625 to 0.0625
- w_value: bfloat16 [8192, 1024], P('gx', 'gy'), may hold values from -0.0625 to 0.0625
- w_output: bfloat16 [4096, 8192], P('gy', 'gx'), may hold values from -0.09375 to 0.09375
- sequence_ids: int32 [2048], P('groups'), parts along dimension 0, may hold values from 0 to 3, as said below
Outputs:
- attention_out: bfloat16 [2048, 8192], P(('groups', 'gy'), 'gx'), parts along dimension 0
There are 2 independent parts, one for each index of `groups`. A program takes and returns all parts, laid end to end along the dimension named above; an argument that names none is the same for every part. Nothing has to cross between parts.
Inputs may be any that keep to these rules, and one draw needn't show every extreme that they name: `tokens`: each token's features carry a per-token and a per-feature scale. `sequence_ids`: never falls along the tokens; each id 0 to 3 names one contiguous run of 1 to 512 tokens, one run exactly 512 long.
All inputs are finite; a program needn't handle non-finite values.
Results may differ from a plain program's by a relative error of at most 0.025.
Values may be sent and summed in bfloat16 or wider, within the bound.
A program may use at most 64 MiB of HBM per device.

v0:
```python
import jax
import jax.numpy as jnp
from jax import lax
from jax.sharding import PartitionSpec as P

D = 8192
HEADS = 32
KV_HEADS = 8
HEAD_DIM = 128


norm_epsilon = 1e-05
rope_base = 500000.0


def sequence_positions(sequence_ids):
    length = sequence_ids.shape[0]
    indices = jnp.arange(length, dtype=jnp.int32)
    starts = jnp.concatenate([jnp.ones((1,), jnp.bool_), sequence_ids[1:] != sequence_ids[:-1]])
    first_rows = lax.cummax(jnp.where(starts, indices, jnp.zeros_like(indices)), axis=0)
    return indices - first_rows


def rotate(values, positions):
    row_count = values.shape[0]
    shaped = values.reshape(row_count, -1, HEAD_DIM)
    half_dim = HEAD_DIM // 2
    inverse = rope_base ** (-(jnp.arange(half_dim, dtype=jnp.float32) * 2.0) / HEAD_DIM)
    angles = positions.astype(jnp.float32)[:, None] * inverse[None, :]
    cosine = jnp.cos(angles)[:, None, :]
    sine = jnp.sin(angles)[:, None, :]
    first = shaped[..., :half_dim]
    second = shaped[..., half_dim:]
    turned = jnp.concatenate(
        [first * cosine - second * sine, second * cosine + first * sine], axis=-1
    )
    return turned.reshape(row_count, -1)


def body(tokens, norm_gain, w_query, w_key, w_value, w_output, sequence_ids):
    length = sequence_ids.shape[0]
    group_size = lax.axis_size("gx")
    row_count = length // group_size
    first_own = lax.axis_index("gx") * row_count
    gain_wide = norm_gain.astype(jnp.float32)[None, :]
    local_rows = tokens.astype(jnp.float32)
    squares = lax.psum(jnp.sum(local_rows * local_rows, axis=1), "gx")
    normed = (local_rows * lax.rsqrt(squares / D + norm_epsilon)[:, None] * gain_wide).astype(
        jnp.bfloat16
    )
    gathered = lax.all_gather(normed, "gy", axis=0, tiled=True)
    positions = sequence_positions(sequence_ids)
    own_positions = lax.dynamic_slice_in_dim(positions, first_own, row_count)
    own_ids = lax.dynamic_slice_in_dim(sequence_ids, first_own, row_count)
    own_index = first_own + jnp.arange(row_count, dtype=jnp.int32)
    query_cols = w_query.shape[1]
    kv_cols = w_key.shape[1]
    groups_here = kv_cols // HEAD_DIM
    per_group = HEADS // KV_HEADS
    scale = 1.0 / jnp.sqrt(jnp.float32(HEAD_DIM))
    joined = jnp.concatenate([w_query, w_key, w_value], axis=1)
    summed = lax.psum_scatter(
        jnp.dot(gathered, joined, preferred_element_type=jnp.float32).astype(jnp.bfloat16),
        "gx",
        scatter_dimension=0,
        tiled=True,
    ).astype(jnp.float32)
    query_rot = rotate(summed[:, :query_cols], own_positions).astype(jnp.bfloat16)
    key_rot = rotate(summed[:, query_cols : query_cols + kv_cols], own_positions).astype(
        jnp.bfloat16
    )
    value_rows = summed[:, query_cols + kv_cols :].astype(jnp.bfloat16)
    query_four = query_rot.reshape(row_count, groups_here, per_group, HEAD_DIM)
    key_piece = lax.all_gather(key_rot, "gx", axis=0, tiled=True)
    value_piece = lax.all_gather(value_rows, "gx", axis=0, tiled=True)
    piece_rows = key_piece.shape[0]
    key_three = key_piece.reshape(piece_rows, groups_here, HEAD_DIM)
    value_three = value_piece.reshape(piece_rows, groups_here, HEAD_DIM)
    scores = (
        jnp.einsum("rgqe,pge->rgqp", query_four, key_three, preferred_element_type=jnp.float32)
        * scale
    )
    key_index = jnp.arange(piece_rows, dtype=jnp.int32)
    allowed = (own_ids[:, None] == sequence_ids[None, :]) & (
        key_index[None, :] <= own_index[:, None]
    )
    weights = jnp.where(allowed[:, None, None, :], jnp.exp(scores), jnp.float32(0.0))
    numerator = jnp.einsum(
        "rgqp,pge->rgqe",
        weights.astype(jnp.bfloat16),
        value_three,
        preferred_element_type=jnp.float32,
    )
    denominator = jnp.sum(weights, axis=-1)
    numerator, denominator = (numerator, denominator)
    attended = (
        (numerator / denominator[..., None]).astype(jnp.bfloat16).reshape(row_count, query_cols)
    )
    partial_value = jnp.dot(
        lax.all_gather(attended, "gx", axis=0, tiled=True),
        w_output,
        preferred_element_type=jnp.float32,
    )
    result = lax.psum_scatter(
        partial_value.astype(jnp.bfloat16), "gy", scatter_dimension=0, tiled=True
    )
    return result


def solution(mesh):
    return jax.shard_map(
        body,
        mesh=mesh,
        in_specs=(
            P(("groups", "gy"), "gx"),
            P("gx"),
            P("gx", "gy"),
            P("gx", "gy"),
            P("gx", "gy"),
            P("gy", "gx"),
            P("groups"),
        ),
        out_specs=P(("groups", "gy"), "gx"),
        check_vma=False,
    )
```

profile of v0, /device:TPU:0, one launch (start us, length us, event | category | flops | bytes accessed | tf_op | source)
XLA Modules:
  0.0 274.9 jit_solution(12898594103326240316)
XLA Ops:
  6.5 1.7 fusion.16
  8.2 13.5 %psum.7 = f32[256]{0:T(256)S(1)} all-reduce(f32[256]{0:T(256)S(1)} %fusion.16), channel_id=1, replica_groups=mesh['groups'=2,'gx'=4,'gy'=4] {'gx'}, use_global_device_ids=true, to_apply=%region_1.0 | all-reduce | flops 256 | bytes 2048 | tf_op jit(solution)/shard_map/psum | solution.py:47
  21.7 0.7 convert_element_type.39
  22.4 2.5 fusion.18
  24.9 32.8 %all-gather.3.cloned.1.call-done = bf16[1024,2048]{1,0:T(8,128)(2,1)} async-done(((bf16[256,2048]{1,0:T(8,128)(2,1)}), bf16[1024,2048]{1,0:T(8,128)(2,1)}) %all-gather.3.cloned.1.call-update) | async-done | bytes 4194320 | tf_op jit(solution)/shard_map/all_gather | solution.py:51
  57.7 11.4 %fusion.13 = bf16[1024,1536]{1,0:T(8,128)(2,1)} fusion(bf16[1024,2048]{1,0:T(8,128)(2,1)} %all-gather.3.cloned.1.call-done, bf16[2048,256]{1,0:T(8,128)(2,1)S(1)} %copy-done.2, bf16[2048,256]{1,0:T(8,128)(2,1)S(1)} %copy-done.3, bf16[2048,1024]{1,0:T(8,128)(2,1)} %param.9), kind=kOutput, calls=%fused_computation.13 | convolution fusion | flops 6462898176 | bytes 13631488 | tf_op jit(solution)/shard_map/dot_general | solution.py:63
  69.4 0.1 add_select_fusion
  69.5 0.3 reduce-window.9
  69.9 0.1 slice_reduce_fusion
  70.2 0.5 multiply_cosine_fusion
  70.7 0.3 fusion.22
  71.0 58.7 %reduce-scatter.3.cloned.1.call-done = bf16[256,1536]{1,0:T(8,128)(2,1)} async-done(((bf16[1024,1536]{1,0:T(8,128)(2,1)}), bf16[256,1536]{1,0:T(8,128)(2,1)}) %reduce-scatter.3.cloned.1.call-update) | async-done | bytes 786448 | tf_op jit(solution)/shard_map/reduce_scatter | solution.py:62
  129.7 1.0 slice.47
  130.7 0.1 reshape.137
  130.8 0.5 subtract_convert_fusion.1
  131.3 0.4 pad_maximum_fusion.1
  131.7 0.1 copy.11
  131.8 15.6 %all_gather.14 = bf16[1024,256]{0,1:T(8,128)(2,1)S(1)} all-gather(bf16[256,256]{0,1:T(8,128)(2,1)S(1)} %bitcast.45), channel_id=1, replica_groups=mesh['groups'=2,'gx'=4,'gy'=4] {'gx'}, dimensions={0}, use_global_device_ids=true | all-gather | bytes 655360 | tf_op jit(solution)/shard_map/all_gather | solution.py:74
  147.4 0.9 slice.46
  148.3 15.3 %all_gather.13 = bf16[1024,256]{1,0:T(8,128)(2,1)S(1)} all-gather(bf16[256,256]{1,0:T(8,128)(2,1)S(1)} %slice.46), channel_id=1, replica_groups=mesh['groups'=2,'gx'=4,'gy'=4] {'gx'}, dimensions={0}, use_global_device_ids=true | all-gather | bytes 655360 | tf_op jit(solution)/shard_map/all_gather | solution.py:75
  163.6 0.2 copy.19
  163.8 0.2 convert_element_type.42
  164.0 0.1 slice_bitcast_fusion
  164.1 0.2 copy.22
  164.3 0.5 subtract_convert_fusion
  164.8 0.3 pad_maximum_fusion
  165.2 2.1 fusion
  167.3 2.5 divide_convert_fusion
  169.8 0.2 reduce-scatter.5.cloned.1.call-start
  170.0 46.1 %all-gather.5.cloned.1.call-done = bf16[1024,1024]{0,1:T(8,128)(2,1)} async-done(((bf16[256,1024]{0,1:T(8,128)(2,1)}), bf16[1024,1024]{0,1:T(8,128)(2,1)}) %all-gather.5.cloned.1.call-update) | async-done | bytes 2097168 | tf_op jit(solution)/shard_map/all_gather | solution.py:100
  216.1 9.3 %convolution_convert_fusion = bf16[1024,2048]{1,0:T(8,128)(2,1)} fusion(bf16[1024,1024]{0,1:T(8,128)(2,1)} %all-gather.5.cloned.1.call-done, bf16[1024,2048]{1,0:T(8,128)(2,1)} %param.12), kind=kOutput, calls=%fused_computation.14 | convolution fusion | flops 4297064448 | bytes 10485760 | tf_op jit(solution)/shard_map/dot_general | solution.py:99
  225.4 42.9 %reduce-scatter.5.cloned.1.call-done = bf16[256,2048]{1,0:T(8,128)(2,1)} async-done(((bf16[1024,2048]{1,0:T(8,128)(2,1)}), bf16[256,2048]{1,0:T(8,128)(2,1)}) %reduce-scatter.5.cloned.1.call-update) | async-done | bytes 1048592 | tf_op jit(solution)/shard_map/reduce_scatter | solution.py:104
  (25 shorter events, 0.7 us)
Async XLA Ops:
  6.5 51.2 %copy-start.2 = (bf16[2048,256]{1,0:T(8,128)(2,1)S(1)}, bf16[2048,256]{1,0:T(8,128)(2,1)}, u32[]{:S(2)}) copy-start(bf16[2048,256]{1,0:T(8,128)(2,1)} %param.11) | copy-start | bytes 3145732
  6.5 51.2 %copy-start.3 = (bf16[2048,256]{1,0:T(8,128)(2,1)S(1)}, bf16[2048,256]{1,0:T(8,128)(2,1)}, u32[]{:S(2)}) copy-start(bf16[2048,256]{1,0:T(8,128)(2,1)} %param.10) | copy-start | bytes 3145732
  6.5 51.2 %all-gather.3.cloned.1.call-start = ((), (), s32[]{:S(2)}) async-start(), calls=%async_computation.2 | async-start | bytes 5242880 | tf_op jit(solution)/shard_map/all_gather | solution.py:51
  24.9 44.4 %copy-start.1 = (s32[1024]{0:T(1024)S(1)}, s32[1024]{0:T(1024)}, u32[]{:S(2)}) copy-start(s32[1024]{0:T(1024)} %param.13) | copy-start | bytes 12292
  24.9 104.8 %reduce-scatter.3.cloned.1.call-start = ((), (), s32[]{:S(2)}) async-start(), calls=%async_computation.3 | async-start | bytes 3932160 | tf_op jit(solution)/shard_map/reduce_scatter | solution.py:62
  69.2 146.9 %all-gather.5.cloned.1.call-start = ((), (), s32[]{:S(2)}) async-start(), calls=%async_computation.4 | async-start | bytes 2621440 | tf_op jit(solution)/shard_map/all_gather | solution.py:100
  129.7 34.1 %copy-start = (bf16[256,1536]{1,0:T(8,128)(2,1)S(1)}, bf16[256,1536]{1,0:T(8,128)(2,1)}, u32[]{:S(2)}) copy-start(bf16[256,1536]{1,0:T(8,128)(2,1)} %reduce-scatter.3.cloned.1.call-done) | copy-start | bytes 2359300
  169.8 98.6 %reduce-scatter.5.cloned.1.call-start = ((), (), s32[]{:S(2)}) async-start(), calls=%async_computation.5 | async-start | bytes 5242880 | tf_op jit(solution)/shard_map/reduce_scatter | solution.py:104
Sparse Core Ops, SparseCore 0:
  25.0 32.6 all-gather.2
  69.3 60.2 reduce-scatter.2
  169.9 46.1 all-gather.4
  225.6 42.7 reduce-scatter.4
where the time goes:
time: 275 us
  waiting for transfers between devices  181 us (66%)
  blocking collectives  44.3 us (16%)
  matrix products  25.3 us (9%)
  between operations  13.3 us (5%)
  other arithmetic  8.15 us (3%)
  local copies, waits for them, and re-layouts  3 us (1%)
    reduce_scatter x1, waiting for transfers between devices, body(): lax.psum_scatter(jnp.dot(gathered, joined, preferred_element_type=jnp.flo...  58.7 us
    all_gather x1, waiting for transfers between devices, body(): lax.all_gather(attended, 'gx', axis=0, tiled=True)  46.1 us
    reduce_scatter x1, waiting for transfers between devices, body(): lax.psum_scatter(partial_value.astype(jnp.bfloat16), 'gy', scatter_dimens...  42.9 us
    all_gather x1, waiting for transfers between devices, body(): gathered = lax.all_gather(normed, 'gy', axis=0, tiled=True)  32.8 us
    all_gather x1, blocking collectives, body(): key_piece = lax.all_gather(key_rot, 'gx', axis=0, tiled=True)  15.6 us
    all_gather x1, blocking collectives, body(): value_piece = lax.all_gather(value_rows, 'gx', axis=0, tiled=True)  15.3 us
    psum x1, blocking collectives, body(): squares = lax.psum(jnp.sum(local_rows * local_rows, axis=1), 'gx')  13.5 us
    dot_general x1, matrix products, body(): jnp.dot(gathered, joined, preferred_element_type=jnp.float32)  11.4 us
  transfers between devices with their start and end apart: 4, of which 4 were waited for; matrix products, arithmetic and copies ran while one was open for 1% of the time, Pallas kernels for 0%

commit v1 on v0

--- a/solution.py
+++ b/solution.py
@@ -44,11 +44,12 @@
     first_own = lax.axis_index("gx") * row_count
     gain_wide = norm_gain.astype(jnp.float32)[None, :]
     local_rows = tokens.astype(jnp.float32)
-    squares = lax.psum(jnp.sum(local_rows * local_rows, axis=1), "gx")
-    normed = (local_rows * lax.rsqrt(squares / D + norm_epsilon)[:, None] * gain_wide).astype(
-        jnp.bfloat16
-    )
-    gathered = lax.all_gather(normed, "gy", axis=0, tiled=True)
+    squares = lax.psum(jnp.sum(local_rows * local_rows, axis=1), ("gx",))
+    inverse_rms = lax.rsqrt(squares / D + norm_epsilon)
+    gained = (local_rows * gain_wide).astype(jnp.bfloat16)
+    gathered = lax.all_gather(gained, "gy", axis=0, tiled=True)
+    all_rms = lax.all_gather(inverse_rms, "gy", axis=0, tiled=True)
+    own_rms = lax.dynamic_slice_in_dim(all_rms, first_own, row_count)
     positions = sequence_positions(sequence_ids)
     own_positions = lax.dynamic_slice_in_dim(positions, first_own, row_count)
     own_ids = lax.dynamic_slice_in_dim(sequence_ids, first_own, row_count)
@@ -64,15 +65,18 @@
         "gx",
         scatter_dimension=0,
         tiled=True,
-    ).astype(jnp.float32)
+    ).astype(jnp.float32) * own_rms[:, None]
     query_rot = rotate(summed[:, :query_cols], own_positions).astype(jnp.bfloat16)
     key_rot = rotate(summed[:, query_cols : query_cols + kv_cols], own_positions).astype(
         jnp.bfloat16
     )
     value_rows = summed[:, query_cols + kv_cols :].astype(jnp.bfloat16)
     query_four = query_rot.reshape(row_count, groups_here, per_group, HEAD_DIM)
-    key_piece = lax.all_gather(key_rot, "gx", axis=0, tiled=True)
-    value_piece = lax.all_gather(value_rows, "gx", axis=0, tiled=True)
+    both = lax.all_gather(
+        jnp.concatenate([key_rot, value_rows], axis=1), "gx", axis=0, tiled=True
+    )
+    key_piece = both[:, :kv_cols]
+    value_piece = both[:, kv_cols:]
     piece_rows = key_piece.shape[0]
     key_three = key_piece.reshape(piece_rows, groups_here, HEAD_DIM)
     value_three = value_piece.reshape(piece_rows, groups_here, HEAD_DIM)

time: 275 us -> 261 us (0.949)
  blocking collectives: 44.3 us -> 16.9 us
  waiting for transfers between devices: 181 us -> 194 us
    all_gather x1 -> x2, waiting for transfers between devices: 32.8 us -> 63.7 us  [the longest x1 37.3 us: body(): gathered = lax.all_gather(gained, 'gy', axis=0, tiled=True)]
    all_gather x2 -> x1, blocking collectives: 30.9 us -> 5.06 us  [body(): all_rms = lax.all_gather(inverse_rms, 'gy', axis=0, tiled=True)]
    reduce_scatter x1, waiting for transfers between devices: 58.7 us -> 42.1 us  [body(): lax.psum_scatter(jnp.dot(gathered, joined, preferred_element_type=jnp.flo...]
  transfers between devices with their start and end apart: 4 -> 5, of which waited for: 4 -> 5; matrix products, arithmetic and copies ran while one was open for 1% -> 1% of each run, Pallas kernels for 0% -> 0%
where the time goes in v1:
time: 261 us
  waiting for transfers between devices  194 us (74%)
  matrix products  25.1 us (10%)
  blocking collectives  16.9 us (6%)
  between operations  13.3 us (5%)
  other arithmetic  8.35 us (3%)
    all_gather x1, waiting for transfers between devices, body(): lax.all_gather(attended, 'gx', axis=0, tiled=True)  45.7 us
    reduce_scatter x1, waiting for transfers between devices, body(): lax.psum_scatter(partial_value.astype(jnp.bfloat16), 'gy', scatter_dimens...  42.9 us
    reduce_scatter x1, waiting for transfers between devices, body(): lax.psum_scatter(jnp.dot(gathered, joined, preferred_element_type=jnp.flo...  42.1 us
    all_gather x1, waiting for transfers between devices, body(): gathered = lax.all_gather(gained, 'gy', axis=0, tiled=True)  37.3 us
    all_gather x1, waiting for transfers between devices, body(): lax.all_gather(jnp.concatenate([key_rot, value_rows], axis=1), 'gx', axis...  26.4 us
    psum x1, blocking collectives, body(): squares = lax.psum(jnp.sum(local_rows * local_rows, axis=1), ('gx',))  11.9 us
    dot_general x1, matrix products, body(): jnp.dot(gathered, joined, preferred_element_type=jnp.float32)  11.4 us
    dot_general x1, matrix products, body(): jnp.dot(lax.all_gather(attended, 'gx', axis=0, tiled=True), w_output, pre...  9.32 us
  transfers between devices with their start and end apart: 5, of which 5 were waited for; matrix products, arithmetic and copies ran while one was open for 1% of the time, Pallas kernels for 0%

profile of v1, /device:TPU:0, one launch (start us, length us, event | category | flops | bytes accessed | tf_op | source)
XLA Modules:
  0.0 261.0 jit_solution(18221360028822627469)
XLA Ops:
  6.5 0.7 convert_element_type.39
  7.2 2.5 fusion.17
  9.8 37.3 %all-gather.5.cloned.1.call-done = bf16[1024,2048]{1,0:T(8,128)(2,1)} async-done(((bf16[256,2048]{1,0:T(8,128)(2,1)}), bf16[1024,2048]{1,0:T(8,128)(2,1)}) %all-gather.5.cloned.1.call-update) | async-done | bytes 4194320 | tf_op jit(solution)/shard_map/all_gather | solution.py:50
  47.1 11.4 %fusion.13 = bf16[1024,1536]{1,0:T(8,128)(2,1)} fusion(bf16[1024,2048]{1,0:T(8,128)(2,1)} %all-gather.5.cloned.1.call-done, bf16[2048,256]{1,0:T(8,128)(2,1)} %param.11, bf16[2048,256]{1,0:T(8,128)(2,1)} %param.10, bf16[2048,1024]{1,0:T(8,128)(2,1)} %param.9), kind=kOutput, calls=%fused_computation.13 | convolution fusion | flops 6462898176 | bytes 13631488 | tf_op jit(solution)/shard_map/dot_general | solution.py:64
  58.7 0.1 add_select_fusion
  58.8 0.3 reduce-window.9
  59.2 11.9 %psum.7 = f32[256]{0:T(256)S(1)} all-reduce(f32[256]{0:T(256)S(1)} %get-tuple-element.9), channel_id=1, replica_groups=mesh['groups'=2,'gx'=4,'gy'=4] {'gx'}, use_global_device_ids=true, to_apply=%region_2.3 | all-reduce | flops 256 | bytes 2048 | tf_op jit(solution)/shard_map/psum | solution.py:47
  71.0 5.1 %all-gather = f32[4,1,256]{2,1,0:T(1,128)S(1)} all-gather(f32[1,1,256]{2,1,0:T(1,128)S(1)} %bitcast.51), channel_id=1, replica_groups=mesh['groups'=2,'gx'=4,'gy'=4] {'gy'}, dimensions={0}, use_global_device_ids=true | all-gather | bytes 5120 | tf_op jit(solution)/shard_map/all_gather | solution.py:51
  76.2 0.1 slice_reduce_fusion
  76.4 0.5 multiply_cosine_fusion
  77.0 42.1 %reduce-scatter.3.cloned.1.call-done = bf16[256,1536]{1,0:T(8,128)(2,1)} async-done(((bf16[1024,1536]{1,0:T(8,128)(2,1)}), bf16[256,1536]{1,0:T(8,128)(2,1)}) %reduce-scatter.3.cloned.1.call-update) | async-done | bytes 786448 | tf_op jit(solution)/shard_map/reduce_scatter | solution.py:63
  119.1 1.3 convert_multiply_fusion.2
  120.4 0.1 reshape.136
  120.6 0.5 subtract_convert_fusion.1
  121.1 0.4 pad_maximum_fusion.2
  121.5 0.7 pad_maximum_fusion.1
  122.3 0.1 dynamic_slice.11
  122.4 0.3 fusion.21
  122.6 0.1 slice_bitcast_fusion
  122.7 0.2 copy.27
  122.9 0.5 subtract_convert_fusion
  123.5 0.3 pad_maximum_fusion
  123.8 26.4 %all-gather.7.cloned.1.call-done = bf16[1024,512]{1,0:T(8,128)(2,1)} async-done(((bf16[256,512]{1,0:T(8,128)(2,1)}), bf16[1024,512]{1,0:T(8,128)(2,1)}) %all-gather.7.cloned.1.call-update) | async-done | bytes 1048592 | tf_op jit(solution)/shard_map/all_gather | solution.py:75
  150.3 1.3 fusion.29
  151.5 0.1 reshape.139
  151.7 0.2 copy.23
  151.9 1.9 fusion
  153.8 2.5 divide_convert_fusion
  156.3 0.2 reduce-scatter.5.cloned.1.call-start
  156.5 45.7 %all-gather.9.cloned.1.call-done = bf16[1024,1024]{0,1:T(8,128)(2,1)} async-done(((bf16[256,1024]{0,1:T(8,128)(2,1)}), bf16[1024,1024]{0,1:T(8,128)(2,1)}) %all-gather.9.cloned.1.call-update) | async-done | bytes 2097168 | tf_op jit(solution)/shard_map/all_gather | solution.py:104
  202.2 9.3 %convolution_convert_fusion = bf16[1024,2048]{1,0:T(8,128)(2,1)} fusion(bf16[1024,1024]{0,1:T(8,128)(2,1)} %all-gather.9.cloned.1.call-done, bf16[1024,2048]{1,0:T(8,128)(2,1)} %param.12), kind=kOutput, calls=%fused_computation.14 | convolution fusion | flops 4297064448 | bytes 10485760 | tf_op jit(solution)/shard_map/dot_general | solution.py:103
  211.5 42.9 %reduce-scatter.5.cloned.1.call-done = bf16[256,2048]{1,0:T(8,128)(2,1)} async-done(((bf16[1024,2048]{1,0:T(8,128)(2,1)}), bf16[256,2048]{1,0:T(8,128)(2,1)}) %reduce-scatter.5.cloned.1.call-update) | async-done | bytes 1048592 | tf_op jit(solution)/shard_map/reduce_scatter | solution.py:108
  (24 shorter events, 0.8 us)
Async XLA Ops:
  6.5 40.5 %all-gather.5.cloned.1.call-start = ((), (), s32[]{:S(2)}) async-start(), calls=%async_computation.2 | async-start | bytes 5242880 | tf_op jit(solution)/shard_map/all_gather | solution.py:50
  9.8 48.9 %copy-start = (s32[1024]{0:T(1024)S(1)}, s32[1024]{0:T(1024)}, u32[]{:S(2)}) copy-start(s32[1024]{0:T(1024)} %param.13) | copy-start | bytes 12292
  9.8 109.3 %reduce-scatter.3.cloned.1.call-start = ((), (), s32[]{:S(2)}) async-start(), calls=%async_computation.3 | async-start | bytes 3932160 | tf_op jit(solution)/shard_map/reduce_scatter | solution.py:63
  58.5 91.7 %all-gather.7.cloned.1.call-start = ((), (), s32[]{:S(2)}) async-start(), calls=%async_computation.4 | async-start | bytes 1310720 | tf_op jit(solution)/shard_map/all_gather | solution.py:75
  122.2 79.9 %all-gather.9.cloned.1.call-start = ((), (), s32[]{:S(2)}) async-start(), calls=%async_computation.5 | async-start | bytes 2621440 | tf_op jit(solution)/shard_map/all_gather | solution.py:104
  156.3 98.1 %reduce-scatter.5.cloned.1.call-start = ((), (), s32[]{:S(2)}) async-start(), calls=%async_computation.6 | async-start | bytes 5242880 | tf_op jit(solution)/shard_map/reduce_scatter | solution.py:108
Sparse Core Ops, SparseCore 0:
  9.9 37.1 all-gather.4
  58.7 60.3 reduce-scatter.2
  122.4 27.8 all-gather.6
  156.4 45.7 all-gather.8
  211.7 42.7 reduce-scatter.4

commit v2 on v1

--- a/solution.py
+++ b/solution.py
@@ -1,6 +1,8 @@
 import jax
 import jax.numpy as jnp
 from jax import lax
+from jax.experimental import pallas as pl
+from jax.experimental.pallas import tpu as pltpu
 from jax.sharding import PartitionSpec as P
 
 D = 8192
@@ -111,9 +113,236 @@
     return result
 
 
+def fused_kernel(
+    tokens_ref, gain_ref, wq_ref, wk_ref, wv_ref, wo_ref, cos_ref, sin_ref, idc_ref, idr_ref,
+    out_ref,
+    xg, ss, ss_in, rms, part, part_in, qs, ks, vs, att, osend, oin,
+    x_s, x_r, ss_s, ss_r, r_s, r_r, p_s, p_r, a_s, a_r, o_s, o_r,
+):
+    rows, feats = tokens_ref.shape
+    f32, bf16 = jnp.float32, jnp.bfloat16
+    mz = lax.axis_index("gx")
+    me = lax.axis_index("gy")
+    chip = me // 2
+    core_at = me - chip * 2
+    core = chip * 2 + 1 - core_at
+    across = (1 - chip) * 2 + core_at
+    diag = (1 - chip) * 2 + 1 - core_at
+    order = [me, core, across, diag]
+    z_to = [lax.rem(mz + o, 4) for o in range(4)]
+    y_to = [lax.rem(me + o, 4) for o in range(4)]
+
+    barrier = pltpu.get_barrier_semaphore()
+    for o in range(1, 4):
+        for where in ({"gx": z_to[o]}, {"gy": y_to[o]}):
+            pl.semaphore_signal(barrier, inc=1, device_id=where, device_id_type=pl.DeviceIdType.MESH)
+    pl.semaphore_wait(barrier, 6)
+
+    def send(src, dst, s, r, where):
+        copy = pltpu.make_async_remote_copy(
+            src_ref=src, dst_ref=dst, send_sem=s, recv_sem=r,
+            device_id=where, device_id_type=pl.DeviceIdType.MESH,
+        )
+        copy.start()
+        return copy
+
+    sent = []
+    step = 64
+
+    @pl.loop(0, rows // step)
+    def _(i):
+        piece = pl.ds(pl.multiple_of(i * step, step), step)
+        wide = tokens_ref[piece, :].astype(f32)
+        xg[me, piece, :] = (wide * gain_ref[...]).astype(bf16)
+        ss[piece, :] = jnp.broadcast_to(jnp.sum(wide * wide, axis=1, keepdims=True), (step, 128))
+
+    to_across = send(xg.at[me], xg.at[me], x_s.at[1], x_r.at[1], {"gy": across})
+    to_core = send(xg.at[me], xg.at[me], x_s.at[0], x_r.at[0], {"gy": core})
+    ss_copies = [
+        send(ss, ss_in.at[o - 1], ss_s.at[o - 1], ss_r.at[o - 1], {"gx": z_to[o]})
+        for o in range(1, 4)
+    ]
+    sent += [to_across, to_core] + ss_copies
+
+    part_copies = []
+
+    def project(j):
+        block = order[j]
+
+        @pl.loop(0, 4)
+        def _(d):
+            cols = pl.ds(pl.multiple_of(d * 256, 256), 256)
+            part[j, d, :, 0:256] = jnp.dot(
+                xg[block], wq_ref[:, cols], preferred_element_type=f32
+            ).astype(bf16)
+
+        for w_ref, at in ((wk_ref, 256), (wv_ref, 384)):
+            both = jnp.dot(xg[block], w_ref[...], preferred_element_type=f32).astype(bf16)
+            for d in range(4):
+                h = d // 2
+                part[j, d, :, at : at + 128] = both[:, h * 128 : h * 128 + 128]
+        part_copies.append([
+            send(part.at[j, z_to[o]], part_in.at[j, o - 1], p_s.at[j, o - 1], p_r.at[j, o - 1],
+                 {"gx": z_to[o]})
+            for o in (1, 3, 2)
+        ])
+
+    project(0)
+    to_core.wait_recv()
+    project(1)
+    for copy in ss_copies:
+        copy.wait_recv()
+    total = ss[...] + ss_in[0] + ss_in[1] + ss_in[2]
+    rms[me] = lax.rsqrt(total / D + norm_epsilon)
+    r_copies = [
+        send(rms.at[me], rms.at[me], r_s.at[o - 1], r_r.at[o - 1], {"gy": y_to[o]})
+        for o in range(1, 4)
+    ]
+    to_across.wait_recv()
+    forward = send(xg.at[across], xg.at[across], x_s.at[2], x_r.at[2], {"gy": core})
+    project(2)
+    forward.wait_recv()
+    project(3)
+    sent += [forward] + r_copies
+    for copy in r_copies:
+        copy.wait_recv()
+
+    for j in range(4):
+        for copy in part_copies[j]:
+            copy.wait_recv()
+        block = order[j]
+        here = pl.ds(pl.multiple_of(block * rows, rows), rows)
+        scale_rows = rms[block]
+        cosine, sine = cos_ref[here, :], sin_ref[here, :]
+        for at in range(0, 512, 128):
+            cols = slice(at, at + 128)
+            value = part[j, mz, :, cols].astype(f32)
+            for o in range(3):
+                value = value + part_in[j, o, :, cols].astype(f32)
+            value = value * scale_rows
+            if at < 384:
+                value = value * cosine + pltpu.roll(value, 64, 1) * sine
+            value = value.astype(bf16)
+            if at < 256:
+                qs[at // 128, here, :] = value
+            elif at == 256:
+                ks[here, :] = value
+            else:
+                vs[here, :] = value
+        sent += part_copies[j]
+
+    att_copies = []
+    length = ks.shape[0]
+    scale = 1.0 / (HEAD_DIM ** 0.5)
+    back = [3, 2, 1, 0]
+    for j in back:
+        block = order[j]
+        here = pl.ds(pl.multiple_of(block * rows, rows), rows)
+        index_q = block * rows + lax.broadcasted_iota(jnp.int32, (rows, length), 0)
+        index_k = lax.broadcasted_iota(jnp.int32, (rows, length), 1)
+        allowed = (idc_ref[here, :] == idr_ref[...]) & (index_k <= index_q)
+        for h in range(2):
+            scores = lax.dot_general(
+                qs[h, here, :], ks[...], (((1,), (1,)), ((), ())), preferred_element_type=f32
+            ) * scale
+            weights = jnp.where(allowed, jnp.exp(scores), 0.0)
+            top = jnp.dot(weights.astype(bf16), vs[...], preferred_element_type=f32)
+            below = jnp.sum(weights, axis=1, keepdims=True)
+            att[j, mz, :, h * 128 : h * 128 + 128] = (top / below).astype(bf16)
+        att_copies.append([
+            send(att.at[j, mz], att.at[j, mz], a_s.at[j, o - 1], a_r.at[j, o - 1], {"gx": z_to[o]})
+            for o in (1, 3, 2)
+        ])
+    o_copies = {}
+    wide_out = wo_ref.shape[1]
+    tile = 512
+    for n, j in enumerate(back):
+        for copy in att_copies[n]:
+            copy.wait_recv()
+        sent += att_copies[n]
+        if j == 2:
+            o_copies[3].wait_recv()
+        if j == 0:
+            o_copies[2].wait_recv()
+            o_copies[1].wait_recv()
+
+        @pl.loop(0, wide_out // tile)
+        def _(i):
+            cols = pl.ds(pl.multiple_of(i * tile, tile), tile)
+            value = jnp.dot(att[j, 0], wo_ref[0:256, cols], preferred_element_type=f32)
+            for d in range(1, 4):
+                value = value + jnp.dot(
+                    att[j, d], wo_ref[d * 256 : d * 256 + 256, cols], preferred_element_type=f32
+                )
+            if j == 2:
+                value = value + oin[2, :, cols].astype(f32)
+            if j == 0:
+                value = value + oin[0, :, cols].astype(f32) + oin[1, :, cols].astype(f32)
+                out_ref[:, cols] = value.astype(bf16)
+            else:
+                osend[j - 1, :, cols] = value.astype(bf16)
+
+        if j > 0:
+            o_copies[j] = send(
+                osend.at[j - 1], oin.at[j - 1], o_s.at[j - 1], o_r.at[j - 1],
+                {"gy": across if j == 2 else core},
+            )
+            sent.append(o_copies[j])
+    for copy in sent:
+        copy.wait_send()
+
+
+def fused_body(tokens, norm_gain, w_query, w_key, w_value, w_output, sequence_ids):
+    length = sequence_ids.shape[0]
+    rows, feats = tokens.shape
+    bf16, f32 = jnp.bfloat16, jnp.float32
+    index = jnp.arange(length, dtype=jnp.int32)
+    earlier = jnp.sum(
+        (sequence_ids[None, :] < sequence_ids[:, None]).astype(jnp.int32), axis=1
+    )
+    positions = index - earlier
+    half = HEAD_DIM // 2
+    inverse = rope_base ** (-(jnp.arange(half, dtype=f32) * 2.0) / HEAD_DIM)
+    angles = positions.astype(f32)[:, None] * inverse[None, :]
+    cosine, sine = jnp.cos(angles), jnp.sin(angles)
+    cosine = jnp.concatenate([cosine, cosine], axis=1)
+    sine = jnp.concatenate([-sine, sine], axis=1)
+    wide_out = w_output.shape[1]
+    dma = pltpu.SemaphoreType.DMA
+    return pl.pallas_call(
+        fused_kernel,
+        out_shape=jax.ShapeDtypeStruct((rows, wide_out), bf16),
+        in_specs=[pl.BlockSpec(memory_space=pltpu.VMEM)] * 10,
+        out_specs=pl.BlockSpec(memory_space=pltpu.VMEM),
+        scratch_shapes=[
+            pltpu.VMEM((4, rows, feats), bf16),
+            pltpu.VMEM((rows, 128), f32),
+            pltpu.VMEM((3, rows, 128), f32),
+            pltpu.VMEM((4, rows, 128), f32),
+            pltpu.VMEM((4, 4, rows, 512), bf16),
+            pltpu.VMEM((4, 3, rows, 512), bf16),
+            pltpu.VMEM((2, length, 128), bf16),
+            pltpu.VMEM((length, 128), bf16),
+            pltpu.VMEM((length, 128), bf16),
+            pltpu.VMEM((4, 4, rows, 256), bf16),
+            pltpu.VMEM((3, rows, wide_out), bf16),
+            pltpu.VMEM((3, rows, wide_out), bf16),
+            dma((3,)), dma((3,)), dma((3,)), dma((3,)), dma((3,)), dma((3,)),
+            dma((4, 3)), dma((4, 3)), dma((4, 3)), dma((4, 3)), dma((3,)), dma((3,)),
+        ],
+        compiler_params=pltpu.CompilerParams(
+            collective_id=0, has_side_effects=True, vmem_limit_bytes=56 * 1024 * 1024
+        ),
+    )(
+        tokens, norm_gain.astype(f32)[None, :], w_query, w_key, w_value, w_output,
+        cosine, sine, sequence_ids[:, None], sequence_ids[None, :],
+    )
+
+
 def solution(mesh):
+    small = mesh.shape["gx"] == 4 and mesh.shape["gy"] == 4
     return jax.shard_map(
-        body,
+        fused_body if small else body,
         mesh=mesh,
         in_specs=(
             P(("groups", "gy"), "gx"),

time: 261 us -> 178 us (0.68)
  waiting for transfers between devices: 194 us -> 0 us
  Pallas kernels: 0 us -> 169 us
  matrix products: 25.1 us -> 0 us
  blocking collectives: 16.9 us -> 0 us
  between operations: 13.3 us -> 0.04 us
  other arithmetic: 8.35 us -> 5.18 us
    pallas_call x0 -> x1, Pallas kernels: none -> 169 us  [fused_body(): pl.pallas_call(fused_kernel, out_shape=jax.ShapeDtypeStruct((rows, wide_o...]
    all_gather x3 -> x0, waiting for transfers between devices: 109 us -> none  [the longest x1 45.7 us: body(): lax.all_gather(attended, 'gx', axis=0, tiled=True)]
    reduce_scatter x2 -> x0, waiting for transfers between devices: 85 us -> none  [the longest x1 42.9 us: body(): lax.psum_scatter(partial_value.astype(jnp.bfloat16), 'gy', scatter_dimens...]
    dot_general x4 -> x0, matrix products: 25.1 us -> none  [the longest x1 11.4 us: body(): jnp.dot(gathered, joined, preferred_element_type=jnp.float32)]
    psum x1 -> x0, blocking collectives: 11.9 us -> none  [body(): squares = lax.psum(jnp.sum(local_rows * local_rows, axis=1), ('gx',))]
    all_gather x1 -> x0, blocking collectives: 5.06 us -> none  [body(): all_rms = lax.all_gather(inverse_rms, 'gy', axis=0, tiled=True)]
  transfers between devices with their start and end apart: 5 -> 0, of which waited for: 5 -> 0; matrix products, arithmetic and copies ran while one was open for 1% -> 0% of each run, Pallas kernels for 0% -> 0%
where the time goes in v2:
time: 178 us
  Pallas kernels  169 us (95%)
  other arithmetic  5.18 us (3%)
  local copies, waits for them, and re-layouts  3.35 us (2%)
    pallas_call x1, Pallas kernels, fused_body(): pl.pallas_call(fused_kernel, out_shape=jax.ShapeDtypeStruct((rows, wide_o...  169 us

profile of v2, /device:TPU:0, one launch (start us, length us, event | category | flops | bytes accessed | tf_op | source)
XLA Modules:
  0.0 177.8 jit_solution(434567174838126173)
XLA Ops:
  0.0 0.0 copy-start
  0.0 0.0 copy-start.1
  0.0 1.3 convert_reduce_fusion
  1.4 1.9 %fusion = (f32[1024,64]{1,0:T(8,128)S(1)}, f32[1024,64]{1,0:T(8,128)S(1)}, f32[1024,64]{1,0:T(8,128)S(1)}) fusion(f32[64]{0:T(128)S(1)} %multiply_power_fusion, f32[1024]{0:T(1024)S(1)} %subtract_convert_fusion), kind=kLoop, calls=%fused_computation.5 | loop fusion | flops 131072 | bytes 790784 | tf_op jit(solution)/shard_map/neg | solution.py:309
  3.3 1.3 pad_maximum_fusion
  4.6 0.0 copy-done
  4.6 1.0 copy.9.idc_ref
  5.7 0.0 copy-done.1
  5.7 0.6 broadcast_in_dim.19
  6.2 169.2 %shard_map.73 = bf16[256,2048]{1,0:T(8,128)(2,1)} custom-call(bf16[256,2048]{1,0:T(8,128)(2,1)} %tokens_ref.1, f32[1,2048]{1,0:T(1,128)} %bitcast.5, bf16[2048,1024]{1,0:T(8,128)(2,1)} %wq_ref.1, bf16[2048,256]{1,0:T(8,128)(2,1)} %wk_ref.1, bf16[2048,256]{1,0:T(8,128)(2,1)} %wv_ref.1, bf16[1024,2048]{1,0:T(8,128)(2,1)} %wo_ref.1, ...), custom_call_target="tpu_custom_call" | custom-call | tf_op jit(solution)/shard_map/pallas_call | solution.py:312
  175.4 2.3 %copy.11 = bf16[256,2048]{1,0:T(8,128)(2,1)} copy(bf16[256,2048]{1,0:T(8,128)(2,1)} %shard_map.73) | data formatting | bytes 2097152
  (2 shorter events, 0.0 us)
Async XLA Ops:
  0.0 4.6 %copy-start = (s32[1024]{0:T(1024)S(1)}, s32[1024]{0:T(1024)}, u32[]{:S(2)}) copy-start(s32[1024]{0:T(1024)} %param.13) | copy-start | bytes 12292
  0.0 5.7 %copy-start.1 = (bf16[2048]{0:T(1024)(128)(2,1)S(1)}, bf16[2048]{0:T(1024)(128)(2,1)}, u32[]{:S(2)}) copy-start(bf16[2048]{0:T(1024)(128)(2,1)} %param.8) | copy-start | bytes 12292

commit v3 on v2

--- a/solution.py
+++ b/solution.py
@@ -116,8 +116,8 @@
 def fused_kernel(
     tokens_ref, gain_ref, wq_ref, wk_ref, wv_ref, wo_ref, cos_ref, sin_ref, idc_ref, idr_ref,
     out_ref,
-    xg, ss, ss_in, rms, part, part_in, qs, ks, vs, att, osend, oin,
-    x_s, x_r, ss_s, ss_r, r_s, r_r, p_s, p_r, a_s, a_r, o_s, o_r,
+    xg, ss, ss_in, rms, part, part_in, qs, kvs, att, osend, oin,
+    x_s, x_r, ss_s, ss_r, r_s, r_r, p_s, p_r, a_s, a_r, o_s, o_r, k_s, k_r,
 ):
     rows, feats = tokens_ref.shape
     f32, bf16 = jnp.float32, jnp.bfloat16
@@ -164,7 +164,39 @@
     ]
     sent += [to_across, to_core] + ss_copies
 
-    part_copies = []
+    sides = [{"gx": lax.rem(mz + 1, 4)}, {"gx": lax.rem(mz + 3, 4)}]
+    parity = lax.rem(mz, 2)
+
+    @pl.when(mz == 0)
+    def _():
+        for j in range(4):
+            part_in[j, 0, 0] = jnp.zeros_like(part_in[j, 0, 0])
+
+    @pl.when(mz == 3)
+    def _():
+        for j in range(4):
+            part_in[j, 1, 3] = jnp.zeros_like(part_in[j, 1, 3])
+
+    def part_copy(j, side, d):
+        return pltpu.make_async_remote_copy(
+            src_ref=part.at[j, d], dst_ref=part_in.at[j, side, d],
+            send_sem=p_s.at[j, side, d], recv_sem=p_r.at[j, side, d],
+            device_id=sides[side], device_id_type=pl.DeviceIdType.MESH,
+        )
+
+    def relay(j):
+        for side, d, here in (
+            (0, 3, (mz == 1) | (mz == 2)), (1, 0, (mz == 1) | (mz == 2)),
+            (0, 2, mz == 1), (1, 1, mz == 2),
+        ):
+            @pl.when(here)
+            def _():
+                copy = part_copy(j, side, d)
+                copy.wait_recv()
+                part[j, d] = (
+                    part[j, d].astype(f32) + part_in[j, side, d].astype(f32)
+                ).astype(bf16)
+                copy.start()
 
     def project(j):
         block = order[j]
@@ -176,16 +208,20 @@
                 xg[block], wq_ref[:, cols], preferred_element_type=f32
             ).astype(bf16)
 
-        for w_ref, at in ((wk_ref, 256), (wv_ref, 384)):
+        for w_ref, odd in ((wk_ref, 0), (wv_ref, 1)):
             both = jnp.dot(xg[block], w_ref[...], preferred_element_type=f32).astype(bf16)
-            for d in range(4):
-                h = d // 2
-                part[j, d, :, at : at + 128] = both[:, h * 128 : h * 128 + 128]
-        part_copies.append([
-            send(part.at[j, z_to[o]], part_in.at[j, o - 1], p_s.at[j, o - 1], p_r.at[j, o - 1],
-                 {"gx": z_to[o]})
-            for o in (1, 3, 2)
-        ])
+            for h in range(2):
+                part[j, 2 * h + odd, :, 256:384] = both[:, h * 128 : h * 128 + 128]
+
+        @pl.when(mz == 0)
+        def _():
+            for d in (3, 2, 1):
+                part_copy(j, 0, d).start()
+
+        @pl.when(mz == 3)
+        def _():
+            for d in (0, 1, 2):
+                part_copy(j, 1, d).start()
 
     project(0)
     to_core.wait_recv()
@@ -198,44 +234,67 @@
         send(rms.at[me], rms.at[me], r_s.at[o - 1], r_r.at[o - 1], {"gy": y_to[o]})
         for o in range(1, 4)
     ]
+    relay(0)
     to_across.wait_recv()
     forward = send(xg.at[across], xg.at[across], x_s.at[2], x_r.at[2], {"gy": core})
     project(2)
+    relay(1)
     forward.wait_recv()
     project(3)
+    relay(2)
     sent += [forward] + r_copies
     for copy in r_copies:
         copy.wait_recv()
 
+    kv_copies = []
     for j in range(4):
-        for copy in part_copies[j]:
-            copy.wait_recv()
+        if j == 3:
+            relay(3)
+
+        @pl.when(mz > 0)
+        def _():
+            part_copy(j, 0, mz).wait_recv()
+
+        @pl.when(mz < 3)
+        def _():
+            part_copy(j, 1, mz).wait_recv()
+
         block = order[j]
         here = pl.ds(pl.multiple_of(block * rows, rows), rows)
         scale_rows = rms[block]
         cosine, sine = cos_ref[here, :], sin_ref[here, :]
-        for at in range(0, 512, 128):
+        for at in range(0, 384, 128):
             cols = slice(at, at + 128)
-            value = part[j, mz, :, cols].astype(f32)
-            for o in range(3):
-                value = value + part_in[j, o, :, cols].astype(f32)
-            value = value * scale_rows
-            if at < 384:
-                value = value * cosine + pltpu.roll(value, 64, 1) * sine
-            value = value.astype(bf16)
+            value = (
+                part[j, mz, :, cols].astype(f32)
+                + part_in[j, 0, mz, :, cols].astype(f32)
+                + part_in[j, 1, mz, :, cols].astype(f32)
+            ) * scale_rows
+            turned = value * cosine + pltpu.roll(value, 64, 1) * sine
             if at < 256:
-                qs[at // 128, here, :] = value
-            elif at == 256:
-                ks[here, :] = value
+                qs[at // 128, here, :] = turned.astype(bf16)
             else:
-                vs[here, :] = value
-        sent += part_copies[j]
-
-    att_copies = []
-    length = ks.shape[0]
+                kvs[parity, here, :] = jnp.where(parity == 0, turned, value).astype(bf16)
+        kv_copies.append(send(
+            kvs.at[parity, here], kvs.at[parity, here], k_s.at[j], k_r.at[j],
+            {"gx": mz + 1 - 2 * parity},
+        ))
+    for copy in kv_copies:
+        copy.wait_recv()
+    sent += kv_copies
+
+    length = kvs.shape[1]
     scale = 1.0 / (HEAD_DIM ** 0.5)
     back = [3, 2, 1, 0]
-    for j in back:
+
+    def att_copy(j, side, source):
+        return pltpu.make_async_remote_copy(
+            src_ref=att.at[j, source], dst_ref=att.at[j, source],
+            send_sem=a_s.at[j, side, source], recv_sem=a_r.at[j, source],
+            device_id=sides[side], device_id_type=pl.DeviceIdType.MESH,
+        )
+
+    def attend(j):
         block = order[j]
         here = pl.ds(pl.multiple_of(block * rows, rows), rows)
         index_q = block * rows + lax.broadcasted_iota(jnp.int32, (rows, length), 0)
@@ -243,23 +302,46 @@
         allowed = (idc_ref[here, :] == idr_ref[...]) & (index_k <= index_q)
         for h in range(2):
             scores = lax.dot_general(
-                qs[h, here, :], ks[...], (((1,), (1,)), ((), ())), preferred_element_type=f32
+                qs[h, here, :], kvs[0], (((1,), (1,)), ((), ())), preferred_element_type=f32
             ) * scale
             weights = jnp.where(allowed, jnp.exp(scores), 0.0)
-            top = jnp.dot(weights.astype(bf16), vs[...], preferred_element_type=f32)
+            top = jnp.dot(weights.astype(bf16), kvs[1], preferred_element_type=f32)
             below = jnp.sum(weights, axis=1, keepdims=True)
             att[j, mz, :, h * 128 : h * 128 + 128] = (top / below).astype(bf16)
-        att_copies.append([
-            send(att.at[j, mz], att.at[j, mz], a_s.at[j, o - 1], a_r.at[j, o - 1], {"gx": z_to[o]})
-            for o in (1, 3, 2)
-        ])
+
+        @pl.when(mz < 3)
+        def _():
+            att_copy(j, 0, mz).start()
+
+        @pl.when(mz > 0)
+        def _():
+            att_copy(j, 1, mz).start()
+
+    def pass_on(j):
+        for source in (1, 2, 0, 3):
+            @pl.when(mz != source)
+            def _():
+                att_copy(j, 0, source).wait_recv()
+
+            if source < 2:
+                @pl.when((mz > source) & (mz < 3))
+                def _():
+                    att_copy(j, 0, source).start()
+            else:
+                @pl.when((mz > 0) & (mz < source))
+                def _():
+                    att_copy(j, 1, source).start()
+
+    attend(3)
+    attend(2)
+    attend(1)
     o_copies = {}
     wide_out = wo_ref.shape[1]
     tile = 512
     for n, j in enumerate(back):
-        for copy in att_copies[n]:
-            copy.wait_recv()
-        sent += att_copies[n]
+        pass_on(j)
+        if j == 3:
+            attend(0)
         if j == 2:
             o_copies[3].wait_recv()
         if j == 0:
@@ -290,6 +372,24 @@
             sent.append(o_copies[j])
     for copy in sent:
         copy.wait_send()
+    for j in range(4):
+        for d in range(4):
+            if d > 0:
+                @pl.when(mz < d)
+                def _():
+                    part_copy(j, 0, d).wait_send()
+            if d < 3:
+                @pl.when(mz > d)
+                def _():
+                    part_copy(j, 1, d).wait_send()
+
+            @pl.when((mz >= d) & (mz < 3))
+            def _():
+                att_copy(j, 0, d).wait_send()
+
+            @pl.when((mz <= d) & (mz > 0))
+            def _():
+                att_copy(j, 1, d).wait_send()
 
 
 def fused_body(tokens, norm_gain, w_query, w_key, w_value, w_output, sequence_ids):
@@ -319,16 +419,16 @@
             pltpu.VMEM((rows, 128), f32),
             pltpu.VMEM((3, rows, 128), f32),
             pltpu.VMEM((4, rows, 128), f32),
-            pltpu.VMEM((4, 4, rows, 512), bf16),
-            pltpu.VMEM((4, 3, rows, 512), bf16),
+            pltpu.VMEM((4, 4, rows, 384), bf16),
+            pltpu.VMEM((4, 2, 4, rows, 384), bf16),
             pltpu.VMEM((2, length, 128), bf16),
-            pltpu.VMEM((length, 128), bf16),
-            pltpu.VMEM((length, 128), bf16),
+            pltpu.VMEM((2, length, 128), bf16),
             pltpu.VMEM((4, 4, rows, 256), bf16),
             pltpu.VMEM((3, rows, wide_out), bf16),
             pltpu.VMEM((3, rows, wide_out), bf16),
             dma((3,)), dma((3,)), dma((3,)), dma((3,)), dma((3,)), dma((3,)),
-            dma((4, 3)), dma((4, 3)), dma((4, 3)), dma((4, 3)), dma((3,)), dma((3,)),
+            dma((4, 2, 4)), dma((4, 2, 4)), dma((4, 2, 4)), dma((4, 4)), dma((3,)), dma((3,)),
+            dma((4,)), dma((4,)),
         ],
         compiler_params=pltpu.CompilerParams(
             collective_id=0, has_side_effects=True, vmem_limit_bytes=56 * 1024 * 1024

time: 178 us -> 145 us (0.81)
  Pallas kernels: 169 us -> 136 us
    pallas_call x1, Pallas kernels: 169 us -> 136 us  [fused_body(): pl.pallas_call(fused_kernel, out_shape=jax.ShapeDtypeStruct((rows, wide_o...]
where the time goes in v3:
time: 145 us
  Pallas kernels  136 us (94%)
  other arithmetic  5.18 us (4%)
  local copies, waits for them, and re-layouts  3.35 us (2%)
    pallas_call x1, Pallas kernels, fused_body(): pl.pallas_call(fused_kernel, out_shape=jax.ShapeDtypeStruct((rows, wide_o...  136 us

profile of v3, /device:TPU:0, one launch (start us, length us, event | category | flops | bytes accessed | tf_op | source)
XLA Modules:
  0.0 145.0 jit_solution(7746242438650794913)
XLA Ops:
  0.0 0.0 copy-start
  0.0 0.0 copy-start.1
  0.0 1.3 convert_reduce_fusion
  1.4 1.9 %fusion = (f32[1024,64]{1,0:T(8,128)S(1)}, f32[1024,64]{1,0:T(8,128)S(1)}, f32[1024,64]{1,0:T(8,128)S(1)}) fusion(f32[64]{0:T(128)S(1)} %multiply_power_fusion, f32[1024]{0:T(1024)S(1)} %subtract_convert_fusion), kind=kLoop, calls=%fused_computation.5 | loop fusion | flops 131072 | bytes 790784 | tf_op jit(solution)/shard_map/neg | solution.py:409
  3.3 1.3 pad_maximum_fusion
  4.6 0.0 copy-done
  4.6 1.0 copy.9.idc_ref
  5.7 0.0 copy-done.1
  5.7 0.6 broadcast_in_dim.19
  6.2 136.4 %shard_map.73 = bf16[256,2048]{1,0:T(8,128)(2,1)} custom-call(bf16[256,2048]{1,0:T(8,128)(2,1)} %tokens_ref.1, f32[1,2048]{1,0:T(1,128)} %bitcast.5, bf16[2048,1024]{1,0:T(8,128)(2,1)} %wq_ref.1, bf16[2048,256]{1,0:T(8,128)(2,1)} %wk_ref.1, bf16[2048,256]{1,0:T(8,128)(2,1)} %wv_ref.1, bf16[1024,2048]{1,0:T(8,128)(2,1)} %wo_ref.1, ...), custom_call_target="tpu_custom_call" | custom-call | tf_op jit(solution)/shard_map/pallas_call | solution.py:412
  142.7 2.3 %copy.11 = bf16[256,2048]{1,0:T(8,128)(2,1)} copy(bf16[256,2048]{1,0:T(8,128)(2,1)} %shard_map.73) | data formatting | bytes 2097152
  (2 shorter events, 0.0 us)
Async XLA Ops:
  0.0 4.6 %copy-start = (s32[1024]{0:T(1024)S(1)}, s32[1024]{0:T(1024)}, u32[]{:S(2)}) copy-start(s32[1024]{0:T(1024)} %param.13) | copy-start | bytes 12292
  0.0 5.7 %copy-start.1 = (bf16[2048]{0:T(1024)(128)(2,1)S(1)}, bf16[2048]{0:T(1024)(128)(2,1)}, u32[]{:S(2)}) copy-start(bf16[2048]{0:T(1024)(128)(2,1)} %param.8) | copy-start | bytes 12292

commit v4 on v3

--- a/solution.py
+++ b/solution.py
@@ -114,10 +114,11 @@
 
 
 def fused_kernel(
-    tokens_ref, gain_ref, wq_ref, wk_ref, wv_ref, wo_ref, cos_ref, sin_ref, idc_ref, idr_ref,
+    tokens_ref, gain_ref, wq_far, wk_far, wv_far, wo_far, inverse_ref, idr_ref,
     out_ref,
     xg, ss, ss_in, rms, part, part_in, qs, kvs, att, osend, oin,
     x_s, x_r, ss_s, ss_r, r_s, r_r, p_s, p_r, a_s, a_r, o_s, o_r, k_s, k_r,
+    wq_ref, wk_ref, wv_ref, wo_ref, w_s, cos_ref, sin_ref, idc_ref,
 ):
     rows, feats = tokens_ref.shape
     f32, bf16 = jnp.float32, jnp.bfloat16
@@ -132,6 +133,14 @@
     z_to = [lax.rem(mz + o, 4) for o in range(4)]
     y_to = [lax.rem(me + o, 4) for o in range(4)]
 
+    loads = [
+        pltpu.make_async_copy(far, near, w_s.at[i])
+        for i, (far, near) in enumerate(
+            ((wq_far, wq_ref), (wk_far, wk_ref), (wv_far, wv_ref), (wo_far, wo_ref))
+        )
+    ]
+    for load in loads:
+        load.start()
     barrier = pltpu.get_barrier_semaphore()
     for o in range(1, 4):
         for where in ({"gx": z_to[o]}, {"gy": y_to[o]}):
@@ -223,6 +232,8 @@
             for d in (0, 1, 2):
                 part_copy(j, 1, d).start()
 
+    for load in loads[:3]:
+        load.wait()
     project(0)
     to_core.wait_recv()
     project(1)
@@ -235,6 +246,25 @@
         for o in range(1, 4)
     ]
     relay(0)
+    ids_row = idr_ref[...].astype(f32)
+    lane = lax.broadcasted_iota(jnp.int32, (128, 128), 1)
+
+    @pl.loop(0, idr_ref.shape[1] // 128)
+    def _(i):
+        piece = pl.ds(pl.multiple_of(i * 128, 128), 128)
+        ids_col = jnp.transpose(
+            jnp.broadcast_to(idr_ref[:, piece].astype(f32), (128, 128))
+        )
+        idc_ref[piece, :] = ids_col
+        earlier = jnp.sum(
+            jnp.where(ids_row < ids_col[:, 0:1], 1.0, 0.0), axis=1, keepdims=True
+        )
+        index = i * 128 + lax.broadcasted_iota(jnp.int32, (128, 128), 0)
+        angles = (index.astype(f32) - earlier) * inverse_ref[...]
+        cos_ref[piece, :] = jnp.cos(angles)
+        sine = jnp.sin(angles)
+        sin_ref[piece, :] = jnp.where(lane < 64, -sine, sine)
+
     to_across.wait_recv()
     forward = send(xg.at[across], xg.at[across], x_s.at[2], x_r.at[2], {"gy": core})
     project(2)
@@ -299,7 +329,7 @@
         here = pl.ds(pl.multiple_of(block * rows, rows), rows)
         index_q = block * rows + lax.broadcasted_iota(jnp.int32, (rows, length), 0)
         index_k = lax.broadcasted_iota(jnp.int32, (rows, length), 1)
-        allowed = (idc_ref[here, :] == idr_ref[...]) & (index_k <= index_q)
+        allowed = (idc_ref[here, 0:1] == ids_row) & (index_k <= index_q)
         for h in range(2):
             scores = lax.dot_general(
                 qs[h, here, :], kvs[0], (((1,), (1,)), ((), ())), preferred_element_type=f32
@@ -336,6 +366,7 @@
     attend(2)
     attend(1)
     o_copies = {}
+    loads[3].wait()
     wide_out = wo_ref.shape[1]
     tile = 512
     for n, j in enumerate(back):
@@ -396,23 +427,17 @@
     length = sequence_ids.shape[0]
     rows, feats = tokens.shape
     bf16, f32 = jnp.bfloat16, jnp.float32
-    index = jnp.arange(length, dtype=jnp.int32)
-    earlier = jnp.sum(
-        (sequence_ids[None, :] < sequence_ids[:, None]).astype(jnp.int32), axis=1
-    )
-    positions = index - earlier
     half = HEAD_DIM // 2
     inverse = rope_base ** (-(jnp.arange(half, dtype=f32) * 2.0) / HEAD_DIM)
-    angles = positions.astype(f32)[:, None] * inverse[None, :]
-    cosine, sine = jnp.cos(angles), jnp.sin(angles)
-    cosine = jnp.concatenate([cosine, cosine], axis=1)
-    sine = jnp.concatenate([-sine, sine], axis=1)
+    inverse = jnp.concatenate([inverse, inverse])[None, :]
     wide_out = w_output.shape[1]
     dma = pltpu.SemaphoreType.DMA
     return pl.pallas_call(
         fused_kernel,
         out_shape=jax.ShapeDtypeStruct((rows, wide_out), bf16),
-        in_specs=[pl.BlockSpec(memory_space=pltpu.VMEM)] * 10,
+        in_specs=[pl.BlockSpec(memory_space=pltpu.VMEM)] * 2
+        + [pl.BlockSpec(memory_space=pl.ANY)] * 4
+        + [pl.BlockSpec(memory_space=pltpu.VMEM)] * 2,
         out_specs=pl.BlockSpec(memory_space=pltpu.VMEM),
         scratch_shapes=[
             pltpu.VMEM((4, rows, feats), bf16),
@@ -429,13 +454,21 @@
             dma((3,)), dma((3,)), dma((3,)), dma((3,)), dma((3,)), dma((3,)),
             dma((4, 2, 4)), dma((4, 2, 4)), dma((4, 2, 4)), dma((4, 4)), dma((3,)), dma((3,)),
             dma((4,)), dma((4,)),
+            pltpu.VMEM(w_query.shape, bf16),
+            pltpu.VMEM(w_key.shape, bf16),
+            pltpu.VMEM(w_value.shape, bf16),
+            pltpu.VMEM(w_output.shape, bf16),
+            dma((4,)),
+            pltpu.VMEM((length, 128), f32),
+            pltpu.VMEM((length, 128), f32),
+            pltpu.VMEM((length, 128), f32),
         ],
         compiler_params=pltpu.CompilerParams(
             collective_id=0, has_side_effects=True, vmem_limit_bytes=56 * 1024 * 1024
         ),
     )(
         tokens, norm_gain.astype(f32)[None, :], w_query, w_key, w_value, w_output,
-        cosine, sine, sequence_ids[:, None], sequence_ids[None, :],
+        inverse, sequence_ids[None, :],
     )
 
 

time: 145 us -> 140 us (0.966)
  other arithmetic: 5.18 us -> 1.97 us
    neg x1 -> x0, other arithmetic: 1.9 us -> none  [fused_body(): sine = jnp.concatenate([-sine, sine], axis=1)]
where the time goes in v4:
time: 140 us
  Pallas kernels  136 us (97%)
  local copies, waits for them, and re-layouts  2.3 us (2%)
  other arithmetic  1.97 us (1%)
    pallas_call x1, Pallas kernels, fused_body(): pl.pallas_call(fused_kernel, out_shape=jax.ShapeDtypeStruct((rows, wide_o...  136 us

profile of v4, /device:TPU:0, one launch (start us, length us, event | category | flops | bytes accessed | tf_op | source)
XLA Modules:
  0.0 140.0 jit_solution(5165030211992956850)
XLA Ops:
  0.0 0.7 maximum_bitcast_fusion.inverse_ref
  0.7 1.3 broadcast_in_dim.15
  2.0 135.7 %shard_map.73 = bf16[256,2048]{1,0:T(8,128)(2,1)} custom-call(bf16[256,2048]{1,0:T(8,128)(2,1)} %tokens_ref.1, f32[1,2048]{1,0:T(1,128)} %bitcast.4, bf16[2048,1024]{1,0:T(8,128)(2,1)} %wq_far.1, bf16[2048,256]{1,0:T(8,128)(2,1)} %wk_far.1, bf16[2048,256]{1,0:T(8,128)(2,1)} %wv_far.1, bf16[1024,2048]{1,0:T(8,128)(2,1)} %wo_far.1, ...), custom_call_target="tpu_custom_call" | custom-call | tf_op jit(solution)/shard_map/pallas_call | solution.py:435
  137.7 2.3 %copy.9 = bf16[256,2048]{1,0:T(8,128)(2,1)} copy(bf16[256,2048]{1,0:T(8,128)(2,1)} %shard_map.73) | data formatting | bytes 2097152
  (1 shorter events, 0.0 us)

commit v5 on v4

--- a/solution.py
+++ b/solution.py
@@ -162,7 +162,7 @@
     def _(i):
         piece = pl.ds(pl.multiple_of(i * step, step), step)
         wide = tokens_ref[piece, :].astype(f32)
-        xg[me, piece, :] = (wide * gain_ref[...]).astype(bf16)
+        xg[me, piece, :] = (wide * gain_ref[...].astype(f32)).astype(bf16)
         ss[piece, :] = jnp.broadcast_to(jnp.sum(wide * wide, axis=1, keepdims=True), (step, 128))
 
     to_across = send(xg.at[me], xg.at[me], x_s.at[1], x_r.at[1], {"gy": across})
@@ -265,10 +265,10 @@
         sine = jnp.sin(angles)
         sin_ref[piece, :] = jnp.where(lane < 64, -sine, sine)
 
+    relay(1)
     to_across.wait_recv()
     forward = send(xg.at[across], xg.at[across], x_s.at[2], x_r.at[2], {"gy": core})
     project(2)
-    relay(1)
     forward.wait_recv()
     project(3)
     relay(2)
@@ -278,7 +278,7 @@
 
     kv_copies = []
     for j in range(4):
-        if j == 3:
+        if j == 2:
             relay(3)
 
         @pl.when(mz > 0)
@@ -364,15 +364,14 @@
 
     attend(3)
     attend(2)
-    attend(1)
     o_copies = {}
     loads[3].wait()
     wide_out = wo_ref.shape[1]
     tile = 512
     for n, j in enumerate(back):
         pass_on(j)
-        if j == 3:
-            attend(0)
+        if j > 1:
+            attend(j - 2)
         if j == 2:
             o_copies[3].wait_recv()
         if j == 0:
@@ -467,7 +466,7 @@
             collective_id=0, has_side_effects=True, vmem_limit_bytes=56 * 1024 * 1024
         ),
     )(
-        tokens, norm_gain.astype(f32)[None, :], w_query, w_key, w_value, w_output,
+        tokens, norm_gain[None, :], w_query, w_key, w_value, w_output,
         inverse, sequence_ids[None, :],
     )
 

time: 140 us -> 146 us (1.043)
  Pallas kernels: 136 us -> 141 us
    pallas_call x1, Pallas kernels: 136 us -> 141 us  [fused_body(): pl.pallas_call(fused_kernel, out_shape=jax.ShapeDtypeStruct((rows, wide_o...]
where the time goes in v5:
time: 146 us; the launch traced here: 145 us
  Pallas kernels  141 us (97%)
  local copies, waits for them, and re-layouts  3.59 us (2%)
    pallas_call x1, Pallas kernels, fused_body(): pl.pallas_call(fused_kernel, out_shape=jax.ShapeDtypeStruct((rows, wide_o...  141 us

profile of v5, /device:TPU:0, one launch (start us, length us, event | category | flops | bytes accessed | tf_op | source)
XLA Modules:
  0.0 145.4 jit_solution(14451910436138714945)
XLA Ops:
  0.0 0.7 maximum_bitcast_fusion.inverse_ref
  0.7 1.3 broadcast_in_dim.9.gain_ref
  2.0 141.1 %shard_map.73 = bf16[256,2048]{1,0:T(8,128)(2,1)} custom-call(bf16[256,2048]{1,0:T(8,128)(2,1)} %tokens_ref.1, bf16[1,2048]{1,0:T(2,128)(2,1)} %broadcast_in_dim.9.gain_ref, bf16[2048,1024]{1,0:T(8,128)(2,1)} %wq_far.1, bf16[2048,256]{1,0:T(8,128)(2,1)} %wk_far.1, bf16[2048,256]{1,0:T(8,128)(2,1)} %wv_far.1, bf16[1024,2048]{1,0:T(8,128)(2,1)} %wo_far.1, ...), custom_call_target="tpu_custom_call" | custom-call | tf_op jit(solution)/shard_map/pallas_call | solution.py:434
  143.1 2.3 %copy.9 = bf16[256,2048]{1,0:T(8,128)(2,1)} copy(bf16[256,2048]{1,0:T(8,128)(2,1)} %shard_map.73) | data formatting | bytes 2097152
  (1 shorter events, 0.0 us)
